TPU v7x, 32 devices: a whole 2x2x4 slice. The times are simulated.
32 devices in a mesh: seq: 8 (over z, x), head: 4 (over y, core).
Axes of the slice: x: 2, y: 2, z: 4, core: 2. Of those that a mesh axis runs over, the one named last changes fastest.
Arguments:
- inputs: float32 [2048, 2048], P('seq'), may hold values from -6 to 6
- gains: float32 [2, 2048], replicated, may hold values from 0.5 to 1.5
- w_proj: bfloat16 [2048, 4, 2048], P(None, None, 'head'), may hold values from -0.125 to 0.125
- w_gates: bfloat16 [2, 2048, 16], P(None, None, 'head'), may hold values from -0.125 to 0.125
- decay: float32 [2, 16], P(None, 'head'), may hold values from -10 to 1
- conv_w: float32 [3, 4, 2048], P(None, None, 'head'), may hold values from -3 to 3
- head_gain: float32 [16, 128], P('head'), may hold values from 0.5 to 1.5
- w_out: bfloat16 [2048, 2048], P('head'), may hold values from -0.25 to 0.25
- w_up: bfloat16 [2048, 2, 5632], P(None, None, 'head'), may hold values from -0.125 to 0.125
- w_down: bfloat16 [5632, 2048], P('head'), may hold values from -0.15625 to 0.15625
- seq_first: int32 [32], P('seq'), may hold values from 0 to 1, as said below
- cotangent: float32 [2048, 2048], P('seq'), may hold values from -6 to 6
Outputs:
- output: float32 [2048, 2048], P('seq')
- grad_inputs: float32 [2048, 2048], P('seq')
- grad_gains: float32 [2, 2048], replicated
- grad_w_proj: float32 [2048, 4, 2048], P('seq', None, 'head')
- grad_w_gates: float32 [2, 2048, 16], P(None, None, 'head')
- grad_decay: float32 [2, 16], P(None, 'head')
- grad_conv_w: float32 [3, 4, 2048], P(None, None, 'head')
- grad_head_gain: float32 [16, 128], P('head')
- grad_w_out: float32 [2048, 2048], P('head', 'seq')
- grad_w_up: float32 [2048, 2, 5632], P('seq', None, 'head')
- grad_w_down: float32 [5632, 2048], P('head', 'seq')
Inputs may be any that keep to these rules, and one draw needn't show every extreme that they name: seq_first[0] is 1. One sequence begins on the first device of seq and ends on the last one.
All inputs are finite; a program needn't handle non-finite values.
Results may differ from a plain program's by a relative error of at most 0.033.
Values may be sent and summed in bfloat16 or wider, within the bound.
A program may use at most 256 MiB of HBM per device.

v0:
```python
from functools import partial

import jax
import jax.numpy as jnp
from jax import lax
from jax.sharding import PartitionSpec as P

GROUP = 64


EPS = 1e-06
HIGH = lax.Precision.HIGHEST


def shifted(array, axis, by):
    length = lax.axis_size(axis)
    pairs = [(i, i + by) for i in range(length) if 0 <= i + by < length]
    return lax.ppermute(array, axis, pairs)


def carried_in(array, axis, join, neutral):
    place = lax.axis_index(axis)
    gathered = jax.tree.map(
        lambda a, kind: lax.all_gather(a.astype(kind), axis), array, (jnp.bfloat16, jnp.bfloat16)
    )
    state = jax.tree.map(lambda a, e: jnp.zeros_like(a) + jnp.asarray(e, a.dtype), array, neutral)

    def carried_one(hop, state):
        return join(
            state,
            jax.tree.map(
                lambda a, own: lax.dynamic_index_in_dim(a, hop, 0, False).astype(own.dtype),
                gathered,
                array,
            ),
        )

    return lax.fori_loop(0, place, carried_one, state)


def prefix_2(array, axis, join, neutral):
    count = lax.axis_size(axis)
    place = lax.axis_index(axis)
    ahead = count - 1 - place
    gathered = jax.tree.map(
        lambda a, kind: lax.all_gather(a.astype(kind), axis),
        array,
        jax.tree.map(lambda a: jnp.bfloat16 if a.dtype == jnp.float32 else a.dtype, array),
    )
    state = jax.tree.map(lambda a, e: jnp.zeros_like(a) + jnp.asarray(e, a.dtype), array, neutral)

    def prefix_one(hop, state):
        source = count - 1 - hop
        return join(
            state,
            jax.tree.map(
                lambda a, own: lax.dynamic_index_in_dim(a, source, 0, False).astype(own.dtype),
                gathered,
                array,
            ),
        )

    return lax.fori_loop(0, ahead, prefix_one, state)


def rms_scale(values, gain):
    return values * lax.rsqrt(jnp.mean(values * values, axis=-1, keepdims=True) + EPS) * gain


def matmul_heads(left, right):
    return jnp.einsum("hij,hjk->hik", left, right, precision=HIGH)


def conv_gates(extended, gate_in, conv_w, decay, first_flags):
    tokens = gate_in.shape[0]
    width = conv_w.shape[1]
    offset = jnp.arange(tokens) % GROUP
    starts = jnp.repeat(first_flags, GROUP).astype(jnp.float32)
    conv_sum = jnp.zeros((tokens,) + extended.shape[1:], jnp.float32)
    for tap_index in range(width):
        keep_tap = 1.0 - starts * (offset < width - 1 - tap_index).astype(jnp.float32)
        conv_sum = (
            conv_sum
            + conv_w[:, tap_index][None]
            * extended[tap_index : tap_index + tokens]
            * keep_tap[:, None, None]
        )
    heads = decay.shape[1]
    activated = jax.nn.silu(conv_sum).reshape(tokens, 3, heads, -1)
    queries = activated[:, 0]
    keys_all = activated[:, 1]
    values = activated[:, 2]
    queries = (
        queries
        * lax.rsqrt(jnp.sum(queries * queries, axis=-1, keepdims=True) + EPS)
        * queries.shape[-1] ** (-0.5)
    )
    keys_all = keys_all * lax.rsqrt(jnp.sum(keys_all * keys_all, axis=-1, keepdims=True) + EPS)
    strength = jax.nn.sigmoid(gate_in[:, 0])
    logdecay = -jnp.exp(decay[0]) * jax.nn.softplus(gate_in[:, 1] + decay[1])
    return (queries, keys_all, values, strength, logdecay)


def to_blocks(array):
    blocks = array.reshape((-1, GROUP) + array.shape[1:])
    return jnp.moveaxis(blocks, 1, 2)


def group_terms(queries, keys_all, values, strength, logdecay):
    query_blocks = to_blocks(queries)
    key_blocks = to_blocks(keys_all)
    value_blocks = to_blocks(values)
    strength_blocks = to_blocks(strength)
    cumulative = jnp.cumsum(to_blocks(logdecay), axis=-1)
    growth = jnp.exp(cumulative)
    size = cumulative.shape[-1]
    lower_strict = jnp.tril(jnp.ones((size, size), jnp.float32), -1)
    lower_incl = jnp.tril(jnp.ones((size, size), jnp.float32))
    spread = cumulative[..., :, None] - cumulative[..., None, :]
    fade_strict = jnp.exp(jnp.where(lower_strict > 0, spread, 0.0)) * lower_strict
    fade_incl = jnp.exp(jnp.where(lower_incl > 0, spread, 0.0)) * lower_incl
    key_gram = jnp.einsum("nhid,nhjd->nhij", key_blocks, key_blocks, precision=HIGH)
    system = (
        jnp.eye(size, dtype=jnp.float32) + strength_blocks[..., :, None] * key_gram * fade_strict
    )
    right = jnp.concatenate(
        [
            strength_blocks[..., None] * key_blocks * growth[..., None],
            strength_blocks[..., None] * value_blocks,
        ],
        axis=-1,
    )
    solved = jax.scipy.linalg.solve_triangular(system, right, lower=True, unit_diagonal=True)
    hdim = key_blocks.shape[-1]
    weights_w = solved[..., :hdim]
    values_u = solved[..., hdim:]
    scores = jnp.einsum("nhid,nhjd->nhij", query_blocks, key_blocks, precision=HIGH) * fade_incl
    key_fade = key_blocks * jnp.exp(cumulative[..., -1:] - cumulative)[..., None]
    query_grow = query_blocks * growth[..., None]
    last_growth = growth[..., -1]
    return (query_grow, scores, weights_w, values_u, key_fade, last_growth)


def state_maps(terms, keep):
    query_grow, scores, weights_w, values_u, key_fade, last_growth = terms
    size = weights_w.shape[-1]
    identity_matrix = jnp.eye(size, dtype=jnp.float32)
    factor = last_growth[..., None, None] * identity_matrix - jnp.einsum(
        "nhcd,nhce->nhde", key_fade, weights_w, precision=HIGH
    )
    offset = jnp.einsum("nhcd,nhce->nhde", key_fade, values_u, precision=HIGH)
    factor = factor * keep[:, None, None, None]

    def compose(carry, item):
        return ((matmul_heads(item[0], carry[0]), matmul_heads(item[0], carry[1]) + item[1]), None)

    start = (
        jnp.broadcast_to(identity_matrix, factor.shape[1:]),
        jnp.zeros(offset.shape[1:], jnp.float32),
    )
    (matrix, constant), unused = lax.scan(compose, start, (factor, offset))
    return (matrix, constant)


def combine(earlier, later):
    return (matmul_heads(later[0], earlier[0]), matmul_heads(later[0], earlier[1]) + later[1])


def core(terms, state_in, keep):

    def advance(state, item):
        query_grow, scores, weights_w, values_u, key_fade, last_growth, keep_one = item
        state = state * keep_one
        fresh = values_u - matmul_heads(weights_w, state)
        result = matmul_heads(query_grow, state) + matmul_heads(scores, fresh)
        state = last_growth[:, None, None] * state + jnp.einsum(
            "hcd,hce->hde", key_fade, fresh, precision=HIGH
        )
        return (state, result)

    state_end, results = lax.scan(advance, state_in, tuple(terms) + (keep,))
    heads = results.shape[1]
    results = jnp.moveaxis(results, 2, 1).reshape(-1, heads, results.shape[-1])
    return (results, state_end)


def out_gate(recurrent, gate_values, head_gain):
    normed = rms_scale(recurrent, head_gain)
    return (normed * jax.nn.silu(gate_values)).reshape(recurrent.shape[0], -1)


def swiglu(gate_up):
    return jax.nn.silu(gate_up[:, 0]) * gate_up[:, 1]


def reduce_weights(rows, cols):
    return (
        (
            lax.psum_scatter(
                rows[0].astype(jnp.bfloat16), "seq", scatter_dimension=0, tiled=True
            ).astype(jnp.float32),
            lax.psum_scatter(
                rows[1].astype(jnp.bfloat16), "seq", scatter_dimension=0, tiled=True
            ).astype(jnp.float32),
        ),
        (
            lax.psum_scatter(
                cols[0].astype(jnp.bfloat16), "seq", scatter_dimension=1, tiled=True
            ).astype(jnp.float32),
            lax.psum_scatter(
                cols[1].astype(jnp.bfloat16), "seq", scatter_dimension=1, tiled=True
            ).astype(jnp.float32),
        ),
    )


def shards(
    inputs,
    gains,
    w_proj,
    w_gates,
    decay,
    conv_w,
    head_gain,
    w_out,
    w_up,
    w_down,
    seq_first,
    cotangent,
):
    tokens = inputs.shape[0]
    heads_here = decay.shape[1]
    hdim = head_gain.shape[1]
    rim_width = conv_w.shape[1] - 1
    normed_in, norm_in_back = jax.vjp(rms_scale, inputs, gains[0])
    normed_low = normed_in.astype(jnp.bfloat16)
    projected = jnp.einsum("td,dkc->tkc", normed_low, w_proj, preferred_element_type=jnp.float32)
    gate_in = jnp.einsum("td,idh->tih", normed_low, w_gates, preferred_element_type=jnp.float32)
    qkv_low = projected[:, :3].astype(jnp.bfloat16)
    rim = shifted(qkv_low[tokens - rim_width :], "seq", 1)
    extended = jnp.concatenate([rim, qkv_low], axis=0).astype(jnp.float32)
    mixed, mixed_back = jax.vjp(
        partial(conv_gates, first_flags=seq_first), extended, gate_in, conv_w, decay
    )
    terms, terms_back = jax.vjp(group_terms, mixed[0], mixed[1], mixed[2], mixed[3], mixed[4])
    keep = 1.0 - seq_first.astype(jnp.float32)
    factors, offsets = state_maps(terms, keep)
    identity = (
        jnp.broadcast_to(jnp.eye(hdim, dtype=jnp.float32), factors.shape),
        jnp.zeros_like(offsets),
    )
    prefix = carried_in((factors, offsets), "seq", combine, identity)
    state_in = prefix[1]
    (recurrent, state_end), core_back = jax.vjp(partial(core, keep=keep), terms, state_in)
    gate_values = projected[:, 3].reshape(tokens, heads_here, hdim)
    gated, gated_back = jax.vjp(out_gate, recurrent, gate_values, head_gain)
    gated_low = gated.astype(jnp.bfloat16)
    attn_part = jnp.dot(gated_low, w_out, preferred_element_type=jnp.float32)
    middle = inputs + lax.psum(attn_part.astype(jnp.bfloat16), "head").astype(jnp.float32)
    normed_mid, norm_mid_back = jax.vjp(rms_scale, middle, gains[1])
    normed_mid_low = normed_mid.astype(jnp.bfloat16)
    gate_up = jnp.einsum("td,dkf->tkf", normed_mid_low, w_up, preferred_element_type=jnp.float32)
    hidden, hidden_back = jax.vjp(swiglu, gate_up)
    hidden_low = hidden.astype(jnp.bfloat16)
    mlp_part = jnp.dot(hidden_low, w_down, preferred_element_type=jnp.float32)
    output = middle + lax.psum(mlp_part.astype(jnp.bfloat16), "head").astype(jnp.float32)
    grad_low = cotangent.astype(jnp.bfloat16)
    grad_down = jnp.einsum("tf,td->fd", hidden_low, grad_low, preferred_element_type=jnp.float32)
    grad_hidden = jnp.einsum("td,fd->tf", grad_low, w_down, preferred_element_type=jnp.float32)
    (grad_gate_up,) = hidden_back(grad_hidden)
    grad_gate_up_low = grad_gate_up.astype(jnp.bfloat16)
    grad_up = jnp.einsum(
        "td,tkf->dkf", normed_mid_low, grad_gate_up_low, preferred_element_type=jnp.float32
    )
    grad_normed_mid = lax.psum(
        jnp.einsum(
            "tkf,dkf->td", grad_gate_up_low, w_up, preferred_element_type=jnp.float32
        ).astype(jnp.bfloat16),
        "head",
    ).astype(jnp.float32)
    grad_middle_norm, grad_gain_mid = norm_mid_back(grad_normed_mid)
    grad_middle = cotangent + grad_middle_norm
    grad_attn_low = grad_middle.astype(jnp.bfloat16)
    grad_wout = jnp.einsum(
        "tc,td->cd", gated_low, grad_attn_low, preferred_element_type=jnp.float32
    )
    grad_gated = jnp.einsum("td,cd->tc", grad_attn_low, w_out, preferred_element_type=jnp.float32)
    grad_recurrent, grad_gate_values, grad_head_gain = gated_back(grad_gated)
    grad_terms_out, local_state_grad = core_back((grad_recurrent, jnp.zeros_like(state_in)))
    suffix = prefix_2((jnp.swapaxes(factors, 1, 2), local_state_grad), "seq", combine, identity)
    grad_terms_state, unused_grad = core_back((jnp.zeros_like(recurrent), suffix[1]))
    grad_terms = jax.tree.map(jnp.add, grad_terms_out, grad_terms_state)
    grad_mixed = terms_back(grad_terms)
    grad_extended, grad_gate_in, grad_conv, grad_decay = mixed_back(grad_mixed)
    rim_grad = shifted(grad_extended[:rim_width], "seq", -1)
    grad_qkv = jnp.concatenate(
        [grad_extended[rim_width:tokens], grad_extended[tokens:] + rim_grad], axis=0
    )
    grad_projected = jnp.concatenate(
        [grad_qkv, grad_gate_values.reshape(tokens, 1, -1)], axis=1
    ).astype(jnp.bfloat16)
    grad_gate_low = grad_gate_in.astype(jnp.bfloat16)
    grad_proj = jnp.einsum(
        "td,tkc->dkc", normed_low, grad_projected, preferred_element_type=jnp.float32
    )
    grad_wgates = jnp.einsum(
        "td,tih->idh", normed_low, grad_gate_low, preferred_element_type=jnp.float32
    )
    grad_normed_part = jnp.einsum(
        "tkc,dkc->td", grad_projected, w_proj, preferred_element_type=jnp.float32
    )
    grad_normed_part = grad_normed_part + jnp.einsum(
        "tih,idh->td", grad_gate_low, w_gates, preferred_element_type=jnp.float32
    )
    grad_normed_in = lax.psum(grad_normed_part.astype(jnp.bfloat16), "head").astype(jnp.float32)
    grad_in_norm, grad_gain_in = norm_in_back(grad_normed_in)
    grad_inputs = grad_middle + grad_in_norm
    summed = (
        lax.psum(grad_conv.astype(jnp.bfloat16), "seq").astype(jnp.float32),
        lax.psum(grad_wgates.astype(jnp.bfloat16), "seq").astype(jnp.float32),
        lax.psum(grad_decay.astype(jnp.bfloat16), "seq").astype(jnp.float32),
        lax.psum(grad_head_gain.astype(jnp.bfloat16), "seq").astype(jnp.float32),
        lax.psum(jnp.stack([grad_gain_in, grad_gain_mid]).astype(jnp.bfloat16), "seq").astype(
            jnp.float32
        ),
    )
    rows_done, cols_done = reduce_weights((grad_proj, grad_up), (grad_wout, grad_down))
    grad_proj_part = rows_done[0]
    grad_up_part = rows_done[1]
    grad_wout_part = cols_done[0]
    grad_down_part = cols_done[1]
    return (
        output,
        grad_inputs,
        summed[4],
        grad_proj_part,
        summed[1],
        summed[2],
        summed[0],
        summed[3],
        grad_wout_part,
        grad_up_part,
        grad_down_part,
    )


def solution(mesh):
    placed = (
        P("seq", None),
        P(),
        P(None, None, "head"),
        P(None, None, "head"),
        P(None, "head"),
        P(None, None, "head"),
        P("head", None),
        P("head", None),
        P(None, None, "head"),
        P("head", None),
        P("seq"),
        P("seq", None),
    )
    return jax.shard_map(
        shards,
        mesh=mesh,
        in_specs=placed,
        out_specs=(
            P("seq", None),
            P("seq", None),
            P(),
            P("seq", None, "head"),
            P(None, None, "head"),
            P(None, "head"),
            P(None, None, "head"),
            P("head", None),
            P("head", "seq"),
            P("seq", None, "head"),
            P("head", "seq"),
        ),
        check_vma=False,
    )
```

profile of v0, /device:TPU:0, one launch (start us, length us, event | category | flops | bytes accessed | tf_op | source)
XLA Modules:
  0.0 1207.0 jit_solution(12628296901425762326)
XLA Ops:
  11.4 8.0 fusion.308
  19.4 4.8 collective-permute-start
  55.1 80.0 %custom-call.10 = f32[4,4,1,64,64]{3,4,2,1,0:T(8,128)} custom-call(f32[4,4,1,64,64]{4,3,2,1,0:T(8,128)} %get-tuple-element.1310), custom_call_target="InvertDiagBlocksLowerTriangular" | custom-call | tf_op jit(solution)/shard_map/jvp(jit(_solve_triangular))/vmap(vmap())/triangular_solve | solution.py:133
  144.5 11.4 while.114
  160.1 37.3 %all-gather.9.cloned.1.call-done = bf16[32,128,128]{2,1,0:T(8,128)(2,1)} async-done(((bf16[4,128,128]{2,1,0:T(8,128)(2,1)}), bf16[32,128,128]{2,1,0:T(8,128)(2,1)}) %all-gather.9.cloned.1.call-update) | async-done | bytes 1048592 | tf_op jit(solution)/shard_map/all_gather | solution.py:24
  197.4 41.6 %all-gather.11.cloned.1.call-done = bf16[32,128,128]{2,1,0:T(8,128)(2,1)} async-done(((bf16[4,128,128]{2,1,0:T(8,128)(2,1)}), bf16[32,128,128]{2,1,0:T(8,128)(2,1)}) %all-gather.11.cloned.1.call-update) | async-done | bytes 1048592 | tf_op jit(solution)/shard_map/all_gather | solution.py:24
  240.8 39.3 %while.111 = (s32[]{:T(128)}, f32[4,128,128]{2,1,0:T(8,128)S(1)}, f32[4,4,64,128]{3,2,1,0:T(8,128)}, f32[4,4,128,128]{3,2,1,0:T(8,128)S(1)}, f32[4,4,64,128]{3,2...) while((s32[]{:T(128)}, f32[4,128,128]{2,1,0:T(8,128)S(1)}, ...), condition=%wide.region_9.10_spmd, body=%wide.region_8.9_spmd.sunk | while | flops 176619520 | bytes 3150561 | solution.py:181
  287.7 49.3 %all-reduce.27.cloned.1.call-done = bf16[256,2048]{1,0:T(8,128)(2,1)} async-done(((bf16[256,2048]{1,0:T(8,128)(2,1)}), bf16[256,2048]{1,0:T(8,128)(2,1)}) %all-reduce.27.cloned.1.call-update) | async-done | bytes 1048592 | tf_op jit(solution)/shard_map/psum | solution.py:259
  339.5 8.2 fusion.131
  352.5 8.4 fusion.149
  366.9 30.8 %all-reduce.29.cloned.1.call-done = bf16[256,2048]{1,0:T(8,128)(2,1)} async-done(((bf16[256,2048]{1,0:T(8,128)(2,1)}), bf16[256,2048]{1,0:T(8,128)(2,1)}) %all-reduce.29.cloned.1.call-update) | async-done | bytes 1048592 | tf_op jit(solution)/shard_map/psum | solution.py:275
  415.6 52.8 %while.115 = (s32[]{:T(128)}, f32[4,128,128]{2,1,0:T(8,128)S(1)}, f32[4,4,64,128]{3,2,1,0:T(8,128)}, f32[4,4,64,64]{3,2,1,0:T(8,128)}, f32[4,4,64,128]{3,2,1,0:T...) while((s32[]{:T(128)}, f32[4,128,128]{2,1,0:T(8,128)S(1)}, ...), condition=%wide.region_19.20_spmd.clone, body=%wide.region_17.19_spmd.clone.sunk | while | flops 353075200 | bytes 5253951 | solution.py:181
  469.2 5.7 convolution_convert_fusion.5
  474.8 35.0 %all-gather.15.cloned.1.call-done = bf16[32,128,128]{2,1,0:T(8,128)(2,1)} async-done(((bf16[4,128,128]{2,1,0:T(8,128)(2,1)}), bf16[32,128,128]{2,1,0:T(8,128)(2,1)}) %all-gather.15.cloned.1.call-update) | async-done | bytes 1048592 | tf_op jit(solution)/shard_map/all_gather | solution.py:46
  509.8 9.4 while.112
  522.7 50.2 %while.113 = (s32[]{:T(128)}, f32[4,128,128]{2,1,0:T(8,128)S(1)}, f32[4,4,64,128]{3,2,1,0:T(8,128)}, f32[4,4,64,64]{3,2,1,0:T(8,128)S(1)}, f32[4,4,64,128]{3,2,1...) while((s32[]{:T(128)}, f32[4,128,128]{2,1,0:T(8,128)S(1)}, ...), condition=%wide.region_24.25_spmd, body=%wide.region_22.24_spmd.sunk | while | flops 352813056 | bytes 4724549 | solution.py:181
  622.0 5.6 convolution_convert_fusion.2
  629.2 8.0 convolution_convert_fusion
  638.4 22.4 %all-reduce.31.cloned.1.call-done = (bf16[256,2048]{1,0:T(8,128)(2,1)}, bf16[256,2048]{1,0:T(8,128)(2,1)}) async-done(((bf16[256,2048]{1,0:T(8,128)(2,1)}, bf16[256,2048]{1,0:T(8,128)(2,1)}), (bf16[256,2048]{1,0:T(8,128)(2,1)}, bf16[256,2048]{1,0:T(8,128)(2,1)})) %all-reduce.31.cloned.1.call-update) | async-done | bytes 2097168 | tf_op jit(solution)/shard_map/psum | solution.py:315
  662.9 38.0 %all-reduce.21 = (bf16[3,4,512]{2,0,1:T(4,128)(2,1)S(1)}, bf16[2,2048]{1,0:T(2,128)(2,1)S(1)}, bf16[2,2048,4]{1,2,0:T(4,128)(2,1)S(1)}, bf16[2,4]{1,0:T(2,128)(2,1)S(1)}, bf16[4,128]{1,0:T(4,128)(2,1)S(1)}) all-reduce(bf16[3,4,512]{2,0,1:T(4,128)(2,1)S(1)} %add_convert_fusion.3, ...), channel_id=1, replica_groups=mesh['seq'=8,'head'=4] {'seq'}, use_global_device_ids=true, to_apply=%region_51.52 | all-reduce | flops 27144 | bytes 108576 | tf_op jit(solution)/shard_map/psum | solution.py:319
  709.3 24.2 %reduce-scatter.7.cloned.1.call-done = bf16[512,256]{1,0:T(8,128)(2,1)} async-done(((bf16[512,2048]{1,0:T(8,128)(2,1)}), bf16[512,256]{1,0:T(8,128)(2,1)}) %reduce-scatter.7.cloned.1.call-update) | async-done | bytes 262160 | tf_op jit(solution)/shard_map/reduce_scatter | solution.py:207
  735.3 111.7 %reduce-scatter.11.cloned.1.call-done = bf16[1408,256]{1,0:T(8,128)(2,1)} async-done(((bf16[1408,2048]{1,0:T(8,128)(2,1)}), bf16[1408,256]{1,0:T(8,128)(2,1)}) %reduce-scatter.11.cloned.1.call-update) | async-done | bytes 720912 | tf_op jit(solution)/shard_map/reduce_scatter | solution.py:210
  849.4 150.9 %reduce-scatter.5.cloned.1.call-done = bf16[256,4,512]{2,0,1:T(8,128)(2,1)} async-done(((bf16[2048,4,512]{2,0,1:T(8,128)(2,1)}), bf16[256,4,512]{2,0,1:T(8,128)(2,1)}) %reduce-scatter.5.cloned.1.call-update) | async-done | bytes 1048592 | tf_op jit(solution)/shard_map/reduce_scatter | solution.py:199
  1003.8 191.8 %reduce-scatter.9.cloned.1.call-done = bf16[256,2,1408]{2,0,1:T(8,128)(2,1)} async-done(((bf16[2048,2,1408]{2,0,1:T(8,128)(2,1)}), bf16[256,2,1408]{2,0,1:T(8,128)(2,1)}) %reduce-scatter.9.cloned.1.call-update) | async-done | bytes 1441808 | tf_op jit(solution)/shard_map/reduce_scatter | solution.py:202
  (629 shorter events, 327.9 us)
Async XLA Ops:
  7.2 278.8 %copy-start = (bf16[512,2048]{1,0:T(8,128)(2,1)S(1)}, bf16[512,2048]{1,0:T(8,128)(2,1)}, u32[]{:S(2)}) copy-start(bf16[512,2048]{1,0:T(8,128)(2,1)} %param.31) | copy-start | bytes 6291460
  7.2 190.2 %all-gather.9.cloned.1.call-start = ((), (), s32[]{:S(2)}) async-start(), calls=%async_computation.10 | async-start | bytes 1179648 | tf_op jit(solution)/shard_map/all_gather | solution.py:24
  19.4 12.4 %collective-permute-start = (bf16[3,3,512]{2,0,1:T(4,128)(2,1)S(1)}, bf16[3,3,512]{2,0,1:T(4,128)(2,1)S(1)}, u32[]{:S(2)}, u32[]{:S(2)}) collective-permute-start(bf16[3,3,512]{2,0,1:T(4,128)(2,1)S(1)} %slice.139), channel_id=1, source_target_pairs={{0,4},{4,8},{8,12},{12,16},{16,20},{20,24},{24,28},{1,5},{5,9},{9,... | collective-permute-start | bytes 27656 | tf_op jit(solution)/shard_map/ppermute | solution.py:18
  40.2 94.9 %copy-start.12 = (f32[256,1,4,128]{3,0,2,1:T(8,128)}, f32[256,1,4,128]{3,0,2,1:T(8,128)S(1)}, u32[]{:S(2)}) copy-start(f32[256,1,4,128]{3,0,2,1:T(8,128)S(1)} %copy.158) | copy-start | bytes 1572868
  41.2 93.9 %copy-start.21 = (f32[256,1,4,128]{3,0,2,1:T(8,128)}, f32[256,1,4,128]{3,0,2,1:T(8,128)S(1)}, u32[]{:S(2)}) copy-start(f32[256,1,4,128]{3,0,2,1:T(8,128)S(1)} %copy.160) | copy-start | bytes 1572868
  156.7 82.3 %all-gather.11.cloned.1.call-start = ((), (), s32[]{:S(2)}) async-start(), calls=%async_computation.11 | async-start | bytes 1179648 | tf_op jit(solution)/shard_map/all_gather | solution.py:24
  157.7 179.4 %all-reduce.27.cloned.1.call-start = ((), (), s32[]{:S(2)}) async-start(), calls=%async_computation.4 | async-start | bytes 2097152 | tf_op jit(solution)/shard_map/psum | solution.py:259
  287.7 51.8 %copy-start.76 = (f32[1,2048]{1,0:T(1,128)S(1)}, f32[1,2048]{1,0:T(1,128)}, u32[]{:S(2)}) copy-start(f32[1,2048]{1,0:T(1,128)} %get-tuple-element.1307) | copy-start | bytes 24580
  287.7 109.9 %all-reduce.29.cloned.1.call-start = ((), (), s32[]{:S(2)}) async-start(), calls=%async_computation.5 | async-start | bytes 2097152 | tf_op jit(solution)/shard_map/psum | solution.py:275
  339.5 61.5 %copy-start.114 = (f32[256]{0:T(256)}, f32[256]{0:T(256)S(1)}, u32[]{:S(2)}) copy-start(f32[256]{0:T(256)S(1)} %fusion.282) | copy-start | bytes 3076
  361.0 113.8 %all-gather.13.cloned.1.call-start = ((), (), s32[]{:S(2)}) async-start(), calls=%async_computation.12 | async-start | bytes 1179648 | tf_op jit(solution)/shard_map/all_gather | solution.py:46
  366.8 143.0 %all-gather.15.cloned.1.call-start = ((), (), s32[]{:S(2)}) async-start(), calls=%async_computation.13 | async-start | bytes 1179648 | tf_op jit(solution)/shard_map/all_gather | solution.py:46
  469.1 191.7 %all-reduce.31.cloned.1.call-start = ((), (), s32[]{:S(2)}) async-start(), calls=%async_computation.14 | async-start | bytes 4194304 | tf_op jit(solution)/shard_map/psum | solution.py:315
  601.1 6.0 collective-permute-start.1
  611.1 122.5 %reduce-scatter.7.cloned.1.call-start = ((), (), s32[]{:S(2)}) async-start(), calls=%async_computation.7 | async-start | bytes 2359296 | tf_op jit(solution)/shard_map/reduce_scatter | solution.py:207
  614.7 232.4 %reduce-scatter.11.cloned.1.call-start = ((), (), s32[]{:S(2)}) async-start(), calls=%async_computation.9 | async-start | bytes 6488064 | tf_op jit(solution)/shard_map/reduce_scatter | solution.py:210
  620.5 379.7 %reduce-scatter.5.cloned.1.call-start = ((), (), s32[]{:S(2)}) async-start(), calls=%async_computation.6 | async-start | bytes 9437184 | tf_op jit(solution)/shard_map/reduce_scatter | solution.py:199
  627.6 568.0 %reduce-scatter.9.cloned.1.call-start = ((), (), s32[]{:S(2)}) async-start(), calls=%async_computation.8 | async-start | bytes 12976128 | tf_op jit(solution)/shard_map/reduce_scatter | solution.py:202
  637.2 23.7 %copy-start.5 = (f32[256,2048]{1,0:T(8,128)S(1)}, f32[256,2048]{1,0:T(8,128)}, u32[]{:S(2)}) copy-start(f32[256,2048]{1,0:T(8,128)} %param.24) | copy-start | bytes 6291460
  637.2 23.6 %copy-start.75 = (f32[1,2048]{1,0:T(1,128)S(1)}, f32[1,2048]{1,0:T(1,128)}, u32[]{:S(2)}) copy-start(f32[1,2048]{1,0:T(1,128)} %copy-done.74) | copy-start | bytes 24580
  638.2 24.7 %copy-start.128 = (bf16[4,128]{1,0:T(4,128)(2,1)S(1)}, bf16[4,128]{1,0:T(4,128)(2,1)}, u32[]{:S(2)}) copy-start(bf16[4,128]{1,0:T(4,128)(2,1)} %get-tuple-element.1136) | copy-start | bytes 3076
  638.2 65.8 %copy-start.117 = (f32[256]{0:T(256)S(1)}, f32[256]{0:T(256)}, u32[]{:S(2)}) copy-start(f32[256]{0:T(256)} %copy-done.116) | copy-start | bytes 3076
  660.8 43.1 %copy-start.60 = (bf16[256,2048]{1,0:T(8,128)(2,1)S(1)}, bf16[256,2048]{1,0:T(8,128)(2,1)}, u32[]{:S(2)}) copy-start(bf16[256,2048]{1,0:T(8,128)(2,1)} %get-tuple-element.1272) | copy-start | bytes 3145732
  1000.3 199.7 %copy-start.1 = (bf16[512,2048]{1,0:T(8,128)(2,1)S(1)}, bf16[512,2048]{1,0:T(8,128)(2,1)}, u32[]{:S(2)}) copy-start(bf16[512,2048]{1,0:T(8,128)(2,1)} %param.31) | copy-start | bytes 6291460
  (127 other events, 476.8 us)
Sparse Core Ops, SparseCore 0:
  156.9 40.4 all-gather.8
  200.1 38.8 all-gather.10
  287.8 49.2 all-reduce.26
  361.1 36.4 all-reduce.28
  399.6 40.5 all-gather.12
  469.2 40.5 all-gather.14
  611.2 49.5 all-reduce.30
  665.3 68.1 reduce-scatter.6
  737.7 109.3 reduce-scatter.10
  851.0 149.2 reduce-scatter.4
  1003.9 191.6 reduce-scatter.8
where the time goes:
time: 1210 us
  waiting for transfers between devices  698 us (58%)
  matrix products  233 us (19%)
  other arithmetic  146 us (12%)
  local copies, waits for them, and re-layouts  66.8 us (6%)
  blocking collectives  38 us (3%)
  between operations  16.2 us (1%)
    reduce_scatter x1, waiting for transfers between devices, reduce_weights(): lax.psum_scatter(rows[1].astype(jnp.bfloat16), 'seq', scatter_dimension=0...  192 us
    reduce_scatter x1, waiting for transfers between devices, reduce_weights(): lax.psum_scatter(rows[0].astype(jnp.bfloat16), 'seq', scatter_dimension=0...  151 us
    dot_general x75, matrix products, matmul_heads(): return jnp.einsum('hij,hjk->hik', left, right, precision=HIGH)  116 us
    reduce_scatter x1, waiting for transfers between devices, reduce_weights(): lax.psum_scatter(cols[1].astype(jnp.bfloat16), 'seq', scatter_dimension=1...  112 us
    another operation x4, other arithmetic, group_terms(): jax.scipy.linalg.solve_triangular(system, right, lower=True, unit_diagona...  81.3 us
    all_gather x2, waiting for transfers between devices, carried_in(): lax.all_gather(a.astype(kind), axis)  78.9 us
    psum x1, waiting for transfers between devices, shards(): lax.psum(attn_part.astype(jnp.bfloat16), 'head').astype(jnp.float32)  49.3 us
    psum x1, blocking collectives, shards(): lax.psum(grad_conv.astype(jnp.bfloat16), 'seq').astype(jnp.float32)  38 us
  transfers between devices with their start and end apart: 13, of which 11 were waited for; matrix products, arithmetic and copies ran while one was open for 11% of the time, Pallas kernels for 0%

commit v1 on v0

--- a/solution.py
+++ b/solution.py
@@ -193,25 +193,53 @@
     return jax.nn.silu(gate_up[:, 0]) * gate_up[:, 1]
 
 
-def reduce_weights(rows, cols):
-    return (
-        (
-            lax.psum_scatter(
-                rows[0].astype(jnp.bfloat16), "seq", scatter_dimension=0, tiled=True
-            ).astype(jnp.float32),
-            lax.psum_scatter(
-                rows[1].astype(jnp.bfloat16), "seq", scatter_dimension=0, tiled=True
-            ).astype(jnp.float32),
-        ),
-        (
-            lax.psum_scatter(
-                cols[0].astype(jnp.bfloat16), "seq", scatter_dimension=1, tiled=True
-            ).astype(jnp.float32),
-            lax.psum_scatter(
-                cols[1].astype(jnp.bfloat16), "seq", scatter_dimension=1, tiled=True
-            ).astype(jnp.float32),
-        ),
-    )
+def across(array, axis, mask):
+    return lax.ppermute(array, axis, [(i, i ^ mask) for i in range(lax.axis_size(axis))])
+
+
+def mirrored(array):
+    return across(array, "seq", lax.axis_size("seq") - 2)
+
+
+def mirrored_shared(array):
+    half = array.shape[0] // 2
+    odd = lax.axis_index("head") % 2
+    mine = mirrored(lax.dynamic_slice_in_dim(array, odd * half, half, 0))
+    other = across(mine, "head", 1)
+    first = jnp.where(odd == 0, mine, other)
+    second = jnp.where(odd == 0, other, mine)
+    return jnp.concatenate([first, second], axis=0)
+
+
+def own_half_columns(array, of):
+    width = array.shape[1] // 2
+    return lax.dynamic_slice_in_dim(array, of * width, width, 1)
+
+
+def sum_in_half(partials):
+    count = len(partials)
+    bits = []
+    bit = 1
+    while bit < count:
+        bits.append(bit)
+        bit *= 2
+    done = []
+    for part, order in ((0, bits), (1, bits[::-1])):
+        held = {}
+        for m in range(count):
+            rows = partials[m].shape[0] // 2
+            held[m] = partials[m][part * rows : (part + 1) * rows]
+        for bit in order:
+            sent = sorted(m for m in held if m & bit)
+            block = jnp.concatenate([held[m].astype(jnp.bfloat16) for m in sent], axis=0)
+            got = across(block, "seq", bit).astype(jnp.float32)
+            rows = got.shape[0] // len(sent)
+            held = {
+                m: held[m] + got[k * rows : (k + 1) * rows]
+                for k, m in enumerate(sorted(m for m in held if not m & bit))
+            }
+        done.append(held[0])
+    return jnp.concatenate(done, axis=0)
 
 
 def shards(
@@ -232,6 +260,19 @@
     heads_here = decay.shape[1]
     hdim = head_gain.shape[1]
     rim_width = conv_w.shape[1] - 1
+    owners = lax.axis_size("seq")
+    place = lax.axis_index("seq")
+    half = place // (owners // 2)
+    masks = range(owners // 2)
+    kept = inputs.shape[1] // owners
+
+    def owned(array, mask):
+        return lax.dynamic_slice_in_dim(array, (place ^ mask) * kept, kept, 1)
+
+    def owned_half(array, mask):
+        within = (place ^ mask) % (owners // 2)
+        return lax.dynamic_slice_in_dim(array, within * kept, kept, 1)
+
     normed_in, norm_in_back = jax.vjp(rms_scale, inputs, gains[0])
     normed_low = normed_in.astype(jnp.bfloat16)
     projected = jnp.einsum("td,dkc->tkc", normed_low, w_proj, preferred_element_type=jnp.float32)
@@ -265,13 +306,36 @@
     mlp_part = jnp.dot(hidden_low, w_down, preferred_element_type=jnp.float32)
     output = middle + lax.psum(mlp_part.astype(jnp.bfloat16), "head").astype(jnp.float32)
     grad_low = cotangent.astype(jnp.bfloat16)
-    grad_down = jnp.einsum("tf,td->fd", hidden_low, grad_low, preferred_element_type=jnp.float32)
     grad_hidden = jnp.einsum("td,fd->tf", grad_low, w_down, preferred_element_type=jnp.float32)
     (grad_gate_up,) = hidden_back(grad_hidden)
     grad_gate_up_low = grad_gate_up.astype(jnp.bfloat16)
-    grad_up = jnp.einsum(
-        "td,tkf->dkf", normed_mid_low, grad_gate_up_low, preferred_element_type=jnp.float32
-    )
+    normed_mid_far = mirrored_shared(normed_mid_low)
+    grad_low_far = mirrored_shared(grad_low)
+    gate_up_far = jnp.einsum(
+        "td,dkf->tkf", normed_mid_far, w_up, preferred_element_type=jnp.float32
+    )
+    grad_hidden_far = jnp.einsum(
+        "td,fd->tf", grad_low_far, w_down, preferred_element_type=jnp.float32
+    )
+    hidden_far, hidden_far_back = jax.vjp(swiglu, gate_up_far)
+    (grad_gate_up_far,) = hidden_far_back(grad_hidden_far)
+    both = lambda near, far: jnp.concatenate([near, far.astype(near.dtype)], axis=0)
+    hidden_both = both(hidden_low, hidden_far)
+    grad_gate_up_both = both(grad_gate_up_low, grad_gate_up_far)
+    normed_mid_both = both(normed_mid_low, normed_mid_far)
+    grad_low_both = both(grad_low, grad_low_far)
+    up_parts = [
+        jnp.einsum(
+            "td,tkf->dkf", owned(normed_mid_both, m), grad_gate_up_both, preferred_element_type=jnp.float32
+        ).astype(jnp.bfloat16)
+        for m in masks
+    ]
+    down_parts = [
+        jnp.einsum(
+            "tf,td->fd", hidden_both, owned(grad_low_both, m), preferred_element_type=jnp.float32
+        ).astype(jnp.bfloat16)
+        for m in masks
+    ]
     grad_normed_mid = lax.psum(
         jnp.einsum(
             "tkf,dkf->td", grad_gate_up_low, w_up, preferred_element_type=jnp.float32
@@ -281,9 +345,15 @@
     grad_middle_norm, grad_gain_mid = norm_mid_back(grad_normed_mid)
     grad_middle = cotangent + grad_middle_norm
     grad_attn_low = grad_middle.astype(jnp.bfloat16)
-    grad_wout = jnp.einsum(
-        "tc,td->cd", gated_low, grad_attn_low, preferred_element_type=jnp.float32
-    )
+    gated_both = both(gated_low, mirrored(gated_low))
+    grad_attn_far = mirrored_shared(own_half_columns(grad_attn_low, 1 - half))
+    grad_attn_both = both(own_half_columns(grad_attn_low, half), grad_attn_far)
+    wout_parts = [
+        jnp.einsum(
+            "tc,td->cd", gated_both, owned_half(grad_attn_both, m), preferred_element_type=jnp.float32
+        ).astype(jnp.bfloat16)
+        for m in masks
+    ]
     grad_gated = jnp.einsum("td,cd->tc", grad_attn_low, w_out, preferred_element_type=jnp.float32)
     grad_recurrent, grad_gate_values, grad_head_gain = gated_back(grad_gated)
     grad_terms_out, local_state_grad = core_back((grad_recurrent, jnp.zeros_like(state_in)))
@@ -300,9 +370,15 @@
         [grad_qkv, grad_gate_values.reshape(tokens, 1, -1)], axis=1
     ).astype(jnp.bfloat16)
     grad_gate_low = grad_gate_in.astype(jnp.bfloat16)
-    grad_proj = jnp.einsum(
-        "td,tkc->dkc", normed_low, grad_projected, preferred_element_type=jnp.float32
-    )
+    normed_far = mirrored_shared(own_half_columns(normed_low, 1 - half))
+    normed_both = both(own_half_columns(normed_low, half), normed_far)
+    grad_projected_both = both(grad_projected, mirrored(grad_projected))
+    proj_parts = [
+        jnp.einsum(
+            "td,tkc->dkc", owned_half(normed_both, m), grad_projected_both, preferred_element_type=jnp.float32
+        ).astype(jnp.bfloat16)
+        for m in masks
+    ]
     grad_wgates = jnp.einsum(
         "td,tih->idh", normed_low, grad_gate_low, preferred_element_type=jnp.float32
     )
@@ -324,11 +400,10 @@
             jnp.float32
         ),
     )
-    rows_done, cols_done = reduce_weights((grad_proj, grad_up), (grad_wout, grad_down))
-    grad_proj_part = rows_done[0]
-    grad_up_part = rows_done[1]
-    grad_wout_part = cols_done[0]
-    grad_down_part = cols_done[1]
+    grad_proj_part = sum_in_half(proj_parts)
+    grad_up_part = sum_in_half(up_parts)
+    grad_wout_part = sum_in_half(wout_parts)
+    grad_down_part = sum_in_half(down_parts)
     return (
         output,
         grad_inputs,

time: 1210 us -> 832 us (0.69)
  waiting for transfers between devices: 698 us -> 213 us
  starting transfers between devices: 7.72 us -> 46.5 us
  other arithmetic: 146 us -> 182 us
    reduce_scatter x4 -> x0, waiting for transfers between devices: 479 us -> none  [the longest x1 192 us: reduce_weights(): lax.psum_scatter(rows[1].astype(jnp.bfloat16), 'seq', scatter_dimension=0...]
    ppermute x0 -> x26, waiting for transfers between devices: none -> 85.9 us  [across(): lax.ppermute(array, axis, [(i, i ^ mask) for i in range(lax.axis_size(axi...]
    ppermute x0 -> x26, starting transfers between devices: none -> 38.2 us  [across(): lax.ppermute(array, axis, [(i, i ^ mask) for i in range(lax.axis_size(axi...]
    all_gather x2, waiting for transfers between devices: 35 us -> 0.01 us  [prefix_2(): lax.all_gather(a.astype(kind), axis)]
    psum x1, waiting for transfers between devices: 49.3 us -> 29.9 us  [shards(): lax.psum(attn_part.astype(jnp.bfloat16), 'head').astype(jnp.float32)]
    psum x1, waiting for transfers between devices: 30.8 us -> 12.2 us  [shards(): lax.psum(jnp.einsum('tkf,dkf->td', grad_gate_up_low, w_up, preferred_elem...]
    psum x1, waiting for transfers between devices: 22.4 us -> 5.7 us  [shards(): lax.psum(grad_normed_part.astype(jnp.bfloat16), 'head').astype(jnp.float32)]
    concatenate x0 -> x17, other arithmetic: none -> 13.6 us  [the longest x4 5.43 us: shards(): jnp.concatenate([near, far.astype(near.dtype)], axis=0)]
  transfers between devices with their start and end apart: 13 -> 35, of which waited for: 11 -> 14; matrix products, arithmetic and copies ran while one was open for 11% -> 36% of each run, Pallas kernels for 0% -> 0%
where the time goes in v1:
time: 832 us; the launch traced here: 823 us
  matrix products  241 us (29%)
  waiting for transfers between devices  213 us (26%)
  other arithmetic  182 us (22%)
  local copies, waits for them, and re-layouts  76 us (9%)
  starting transfers between devices  46.5 us (6%)
  blocking collectives  46.2 us (6%)
  between operations  17.1 us (2%)
    dot_general x75, matrix products, matmul_heads(): return jnp.einsum('hij,hjk->hik', left, right, precision=HIGH)  116 us
    ppermute x26, waiting for transfers between devices, across(): lax.ppermute(array, axis, [(i, i ^ mask) for i in range(lax.axis_size(axi...  85.9 us
    another operation x4, other arithmetic, group_terms(): jax.scipy.linalg.solve_triangular(system, right, lower=True, unit_diagona...  81.3 us
    all_gather x2, waiting for transfers between devices, carried_in(): lax.all_gather(a.astype(kind), axis)  77.8 us
    psum x1, blocking collectives, shards(): lax.psum(grad_conv.astype(jnp.bfloat16), 'seq').astype(jnp.float32)  46.2 us
    ppermute x26, starting transfers between devices, across(): lax.ppermute(array, axis, [(i, i ^ mask) for i in range(lax.axis_size(axi...  38.2 us
    dot_general x20, matrix products, advance(): jnp.einsum('hcd,hce->hde', key_fade, fresh, precision=HIGH)  34 us
    psum x1, waiting for transfers between devices, shards(): lax.psum(attn_part.astype(jnp.bfloat16), 'head').astype(jnp.float32)  29.9 us
  transfers between devices with their start and end apart: 35, of which 14 were waited for; matrix products, arithmetic and copies ran while one was open for 36% of the time, Pallas kernels for 0%

profile of v1, /device:TPU:0, one launch (start us, length us, event | category | flops | bytes accessed | tf_op | source)
XLA Modules:
  0.0 823.3 jit_solution(3097643969526757730)
XLA Ops:
  11.5 8.0 fusion.374
  20.1 5.4 collective-permute-start
  57.6 80.0 %custom-call.10 = f32[4,4,1,64,64]{3,4,2,1,0:T(8,128)} custom-call(f32[4,4,1,64,64]{4,3,2,1,0:T(8,128)} %get-tuple-element.1339), custom_call_target="InvertDiagBlocksLowerTriangular" | custom-call | tf_op jit(solution)/shard_map/jvp(jit(_solve_triangular))/vmap(vmap())/triangular_solve | solution.py:133
  147.1 11.4 %while.114 = (s32[]{:T(128)}, f32[4,128,128]{2,1,0:T(8,128)S(1)}, f32[4,128,128]{2,1,0:T(8,128)S(1)}, f32[4,4,128,128]{3,2,1,0:T(8,128)}, f32[4,4,128,128]{3,2,1,0:T(8,128)}, /*index=5*/s32[]{:T(128)}, s32[]{:T(128)}) while((s32[]{:T(128)}, f32[4,128,128]{2,1,0:T(8,128)S(1)}, f32[4,128,128]{2,1,0:T(8,128)S(1)}, ...), condition=%wide.region_4.5_spmd.clone, body=%wide.region_3.4_spmd.clone.sunk | while | flops 201457664 | bytes 2885218 | solution.py:161
  162.6 36.8 %all-gather.9.cloned.1.call-done = bf16[32,128,128]{2,1,0:T(8,128)(2,1)} async-done(((bf16[4,128,128]{2,1,0:T(8,128)(2,1)}), bf16[32,128,128]{2,1,0:T(8,128)(2,1)}) %all-gather.9.cloned.1.call-update) | async-done | bytes 1048592 | tf_op jit(solution)/shard_map/all_gather | solution.py:24
  199.4 41.1 %all-gather.11.cloned.1.call-done = bf16[32,128,128]{2,1,0:T(8,128)(2,1)} async-done(((bf16[4,128,128]{2,1,0:T(8,128)(2,1)}), bf16[32,128,128]{2,1,0:T(8,128)(2,1)}) %all-gather.11.cloned.1.call-update) | async-done | bytes 1048592 | tf_op jit(solution)/shard_map/all_gather | solution.py:24
  242.2 39.3 %while.111 = (s32[]{:T(128)}, f32[4,128,128]{2,1,0:T(8,128)S(1)}, f32[4,4,64,128]{3,2,1,0:T(8,128)}, f32[4,4,128,128]{3,2,1,0:T(8,128)S(1)}, f32[4,4,64,128]{3,2...) while((s32[]{:T(128)}, f32[4,128,128]{2,1,0:T(8,128)S(1)}, ...), condition=%wide.region_9.10_spmd, body=%wide.region_8.9_spmd.sunk | while | flops 176619520 | bytes 3150561 | solution.py:181
  291.3 14.5 %collective-permute-start.2 = (bf16[128,1024]{1,0:T(8,128)(2,1)S(1)}, bf16[128,1024]{1,0:T(8,128)(2,1)}, u32[]{:S(2)}, u32[]{:S(2)}) collective-permute-start(bf16[128,1024]{1,0:T(8,128)(2,1)S(1)} %dynamic_slice.280), channel_id=1, source_target_pairs={{0,24},{4,28},{8,16},{12,20},{16,8},{20,12},{24,0},{28,4},{1,25},{... | collective-permute-start | bytes 786440 | tf_op jit(solution)/shard_map/ppermute | solution.py:197
  309.3 29.9 %all-reduce.29.cloned.1.call-done = bf16[256,2048]{1,0:T(8,128)(2,1)} async-done(((bf16[256,2048]{1,0:T(8,128)(2,1)}), bf16[256,2048]{1,0:T(8,128)(2,1)}) %all-reduce.29.cloned.1.call-update) | async-done | bytes 1048592 | tf_op jit(solution)/shard_map/psum | solution.py:300
  342.5 8.1 fusion.133
  355.1 4.2 fusion.151
  377.9 5.4 convolution_convert_fusion.9
  383.9 12.2 %all-reduce.31.cloned.1.call-done = bf16[256,2048]{1,0:T(8,128)(2,1)} async-done(((bf16[256,2048]{1,0:T(8,128)(2,1)}), bf16[256,2048]{1,0:T(8,128)(2,1)}) %all-reduce.31.cloned.1.call-update) | async-done | bytes 1048592 | tf_op jit(solution)/shard_map/psum | solution.py:339
  419.4 52.8 %while.115 = (s32[]{:T(128)}, f32[4,128,128]{2,1,0:T(8,128)S(1)}, f32[4,4,64,128]{3,2,1,0:T(8,128)}, f32[4,4,64,64]{3,2,1,0:T(8,128)}, f32[4,4,64,128]{3,2,1,0:T...) while((s32[]{:T(128)}, f32[4,128,128]{2,1,0:T(8,128)S(1)}, ...), condition=%wide.region_19.20_spmd.clone, body=%wide.region_17.19_spmd.clone.sunk | while | flops 353075200 | bytes 5253951 | solution.py:181
  478.5 7.7 fusion.129
  515.9 41.1 %collective-permute-done.24 = bf16[1408,256]{1,0:T(8,128)(2,1)S(1)} collective-permute-done((bf16[1408,256]{1,0:T(8,128)(2,1)S(1)}, bf16[1408,256]{1,0:T(8,128)(2,1)S(1)}, u32[]{:S(2)}, u32[]{:S(2)}) %collective-permute-start.24) | collective-permute-done | bytes 720928 | tf_op jit(solution)/shard_map/ppermute | solution.py:197
  566.5 5.5 collective-permute-done.25
  575.9 9.2 %while.112 = (s32[]{:T(128)}, f32[4,128,128]{2,1,0:T(8,128)S(1)}, s32[]{:T(128)}, bf16[8,4,128,128]{3,2,1,0:T(8,128)(2,1)}, bf16[8,4,128,128]{3,2,1,0:T(8,128)(2...) while((s32[]{:T(128)}, f32[4,128,128]{2,1,0:T(8,128)S(1)}, s32[]{:T(128)}, ...), condition=%wide.region_21.22_spmd, body=%wide.region_20.21_spmd.sunk | while | flops 100794376 | bytes 1311891 | solution.py:63
  588.6 50.1 %while.113 = (s32[]{:T(128)}, f32[4,128,128]{2,1,0:T(8,128)S(1)}, f32[4,4,64,128]{3,2,1,0:T(8,128)}, f32[4,4,64,64]{3,2,1,0:T(8,128)S(1)}, f32[4,4,64,128]{3,2,1...) while((s32[]{:T(128)}, f32[4,128,128]{2,1,0:T(8,128)S(1)}, ...), condition=%wide.region_24.25_spmd, body=%wide.region_22.24_spmd.sunk | while | flops 352813056 | bytes 4724549 | solution.py:181
  669.5 4.2 pad_add_fusion
  690.3 5.0 fusion.148
  695.4 26.7 %collective-permute-done.21 = bf16[128,2,1408]{2,0,1:T(8,128)(2,1)} collective-permute-done((bf16[128,2,1408]{2,0,1:T(8,128)(2,1)}, bf16[128,2,1408]{2,0,1:T(8,128)(2,1)}, u32[]{:S(2)}, u32[]{:S(2)}) %collective-permute-start.21) | collective-permute-done | bytes 720928 | tf_op jit(solution)/shard_map/ppermute | solution.py:197
  740.9 5.7 all-reduce.33.cloned.1.call-done
  748.5 46.2 %all-reduce.23 = (bf16[3,4,512]{2,0,1:T(4,128)(2,1)S(1)}, bf16[2,2048]{1,0:T(2,128)(2,1)S(1)}, bf16[2,2048,4]{1,2,0:T(4,128)(2,1)S(1)}, bf16[2,4]{1,0:T(2,128)(2,1)S(1)}, bf16[4,128]{1,0:T(4,128)(2,1)S(1)}) all-reduce(bf16[3,4,512]{2,0,1:T(4,128)(2,1)S(1)} %add_convert_fusion.2, ...), channel_id=1, replica_groups=mesh['seq'=8,'head'=4] {'seq'}, use_global_device_ids=true, to_apply=%region_50.51 | all-reduce | flops 27144 | bytes 108576 | tf_op jit(solution)/shard_map/psum | solution.py:395
  (803 shorter events, 417.7 us)
Async XLA Ops:
  7.2 192.2 %all-gather.9.cloned.1.call-start = ((), (), s32[]{:S(2)}) async-start(), calls=%async_computation.2 | async-start | bytes 1179648 | tf_op jit(solution)/shard_map/all_gather | solution.py:24
  159.3 81.1 %all-gather.11.cloned.1.call-start = ((), (), s32[]{:S(2)}) async-start(), calls=%async_computation.3 | async-start | bytes 1179648 | tf_op jit(solution)/shard_map/all_gather | solution.py:24
  160.0 179.2 %all-reduce.29.cloned.1.call-start = ((), (), s32[]{:S(2)}) async-start(), calls=%async_computation | async-start | bytes 2097152 | tf_op jit(solution)/shard_map/psum | solution.py:300
  290.1 106.0 %all-reduce.31.cloned.1.call-start = ((), (), s32[]{:S(2)}) async-start(), calls=%async_computation.1 | async-start | bytes 2097152 | tf_op jit(solution)/shard_map/psum | solution.py:339
  291.3 68.1 %collective-permute-start.2 = (bf16[128,1024]{1,0:T(8,128)(2,1)S(1)}, bf16[128,1024]{1,0:T(8,128)(2,1)}, u32[]{:S(2)}, u32[]{:S(2)}) collective-permute-start(bf16[128,1024]{1,0:T(8,128)(2,1)S(1)} %dynamic_slice.280), channel_id=1, source_target_pairs={{0,24},{4,28},{8,16},{12,20},{16,8},{20,12},{24,0},{28,4},{1,25},{... | collective-permute-start | bytes 786440 | tf_op jit(solution)/shard_map/ppermute | solution.py:197
  309.3 54.1 %collective-permute-start.18 = (bf16[128,2048]{1,0:T(8,128)(2,1)}, bf16[128,2048]{1,0:T(8,128)(2,1)}, u32[]{:S(2)}, u32[]{:S(2)}) collective-permute-start(bf16[128,2048]{1,0:T(8,128)(2,1)} %constant_dynamic-slice_fusion.3), channel_id=1, source_target_pairs={{0,24},{4,28},{8,16},{12,20},{16,8},{20,12},{24,0},{28,4},{1,25},{... | collective-permute-start | bytes 1572872 | tf_op jit(solution)/shard_map/ppermute | solution.py:197
  359.3 216.6 %all-gather.13.cloned.1.call-start = ((), (), s32[]{:S(2)}) async-start(), calls=%async_computation.4 | async-start | bytes 1179648 | tf_op jit(solution)/shard_map/all_gather | solution.py:46
  367.2 208.7 %all-gather.15.cloned.1.call-start = ((), (), s32[]{:S(2)}) async-start(), calls=%async_computation.5 | async-start | bytes 1179648 | tf_op jit(solution)/shard_map/all_gather | solution.py:46
  373.7 121.9 %collective-permute-start.9 = (bf16[256,512]{1,0:T(8,128)(2,1)}, bf16[256,512]{1,0:T(8,128)(2,1)}, u32[]{:S(2)}, u32[]{:S(2)}) collective-permute-start(bf16[256,512]{1,0:T(8,128)(2,1)} %fusion.257), channel_id=1, source_target_pairs={{0,24},{4,28},{8,16},{12,20},{16,8},{20,12},{24,0},{28,4},{1,25},{... | collective-permute-start | bytes 786440 | tf_op jit(solution)/shard_map/ppermute | solution.py:197
  383.3 31.7 %collective-permute-start.16 = (bf16[128,2048]{1,0:T(8,128)(2,1)}, bf16[128,2048]{1,0:T(8,128)(2,1)}, u32[]{:S(2)}, u32[]{:S(2)}) collective-permute-start(bf16[128,2048]{1,0:T(8,128)(2,1)} %constant_dynamic-slice_fusion.4), channel_id=1, source_target_pairs={{0,24},{4,28},{8,16},{12,20},{16,8},{20,12},{24,0},{28,4},{1,25},{... | collective-permute-start | bytes 1572872 | tf_op jit(solution)/shard_map/ppermute | solution.py:197
  409.2 65.9 %collective-permute-start.10 = (bf16[128,1024]{1,0:T(8,128)(2,1)}, bf16[128,1024]{1,0:T(8,128)(2,1)S(1)}, u32[]{:S(2)}, u32[]{:S(2)}) collective-permute-start(bf16[128,1024]{1,0:T(8,128)(2,1)} %dynamic_slice.286), channel_id=1, source_target_pairs={{0,24},{4,28},{8,16},{12,20},{16,8},{20,12},{24,0},{28,4},{1,25},{... | collective-permute-start | bytes 786440 | tf_op jit(solution)/shard_map/ppermute | solution.py:197
  415.0 60.6 %collective-permute-start.17 = (bf16[128,2048]{1,0:T(8,128)(2,1)}, bf16[128,2048]{1,0:T(8,128)(2,1)}, u32[]{:S(2)}, u32[]{:S(2)}) collective-permute-start(bf16[128,2048]{1,0:T(8,128)(2,1)} %collective-permute-done.16), channel_id=1, source_target_pairs={{0,1},{1,0},{2,3},{3,2},{4,5},{5,4},{6,7},{7,6},{8,9},{9,8},{10,11... | collective-permute-start | bytes 1572872 | tf_op jit(solution)/shard_map/ppermute | solution.py:197
  473.5 273.1 %all-reduce.33.cloned.1.call-start = ((), (), s32[]{:S(2)}) async-start(), calls=%async_computation.6 | async-start | bytes 4194304 | tf_op jit(solution)/shard_map/psum | solution.py:391
  475.0 18.9 %collective-permute-start.11 = (bf16[128,1024]{1,0:T(8,128)(2,1)S(1)}, bf16[128,1024]{1,0:T(8,128)(2,1)S(1)}, u32[]{:S(2)}, u32[]{:S(2)}) collective-permute-start(bf16[128,1024]{1,0:T(8,128)(2,1)S(1)} %collective-permute-done.10), channel_id=1, source_target_pairs={{0,1},{1,0},{2,3},{3,2},{4,5},{5,4},{6,7},{7,6},{8,9},{9,8},{10,11... | collective-permute-start | bytes 786440 | tf_op jit(solution)/shard_map/ppermute | solution.py:197
  505.4 175.6 %collective-permute-start.20 = (bf16[256,2,1408]{2,0,1:T(8,128)(2,1)}, bf16[256,2,1408]{2,0,1:T(8,128)(2,1)}, u32[]{:S(2)}, u32[]{:S(2)}) collective-permute-start(bf16[256,2,1408]{2,0,1:T(8,128)(2,1)} %pad_maximum_fusion.6), channel_id=1, source_target_pairs={{0,4},{4,0},{8,12},{12,8},{16,20},{20,16},{24,28},{28,24},{1,5},{5... | collective-permute-start | bytes 4325384 | tf_op jit(solution)/shard_map/ppermute | solution.py:197
  506.7 178.0 %collective-permute-start.22 = (bf16[256,2,1408]{2,0,1:T(8,128)(2,1)}, bf16[256,2,1408]{2,0,1:T(8,128)(2,1)}, u32[]{:S(2)}, u32[]{:S(2)}) collective-permute-start(bf16[256,2,1408]{2,0,1:T(8,128)(2,1)} %pad_maximum_fusion.7), channel_id=1, source_target_pairs={{0,8},{4,12},{8,0},{12,4},{16,24},{20,28},{24,16},{28,20},{1,9},{5... | collective-permute-start | bytes 4325384 | tf_op jit(solution)/shard_map/ppermute | solution.py:197
  509.7 47.3 %collective-permute-start.24 = (bf16[1408,256]{1,0:T(8,128)(2,1)S(1)}, bf16[1408,256]{1,0:T(8,128)(2,1)S(1)}, u32[]{:S(2)}, u32[]{:S(2)}) collective-permute-start(bf16[1408,256]{1,0:T(8,128)(2,1)S(1)} %pad_maximum_fusion.15), channel_id=1, source_target_pairs={{0,4},{4,0},{8,12},{12,8},{16,20},{20,16},{24,28},{28,24},{1,5},{5... | collective-permute-start | bytes 2162696 | tf_op jit(solution)/shard_map/ppermute | solution.py:197
  513.2 48.5 %collective-permute-start.26 = (bf16[1408,256]{1,0:T(8,128)(2,1)S(1)}, bf16[1408,256]{1,0:T(8,128)(2,1)S(1)}, u32[]{:S(2)}, u32[]{:S(2)}) collective-permute-start(bf16[1408,256]{1,0:T(8,128)(2,1)S(1)} %pad_maximum_fusion.16), channel_id=1, source_target_pairs={{0,8},{4,12},{8,0},{12,4},{16,24},{20,28},{24,16},{28,20},{1,9},{5... | collective-permute-start | bytes 2162696 | tf_op jit(solution)/shard_map/ppermute | solution.py:197
  515.4 49.1 %collective-permute-start.13 = (bf16[256,256]{1,0:T(8,128)(2,1)S(1)}, bf16[256,256]{1,0:T(8,128)(2,1)S(1)}, u32[]{:S(2)}, u32[]{:S(2)}) collective-permute-start(bf16[256,256]{1,0:T(8,128)(2,1)S(1)} %fusion.265), channel_id=1, source_target_pairs={{0,8},{4,12},{8,0},{12,4},{16,24},{20,28},{24,16},{28,20},{1,9},{5... | collective-permute-start | bytes 393224 | tf_op jit(solution)/shard_map/ppermute | solution.py:197
  681.0 48.1 %collective-permute-start.4 = (bf16[256,4,512]{2,0,1:T(8,128)(2,1)}, bf16[256,4,512]{2,0,1:T(8,128)(2,1)}, u32[]{:S(2)}, u32[]{:S(2)}) collective-permute-start(bf16[256,4,512]{2,0,1:T(8,128)(2,1)} %pad_maximum_fusion.10), channel_id=1, source_target_pairs={{0,24},{4,28},{8,16},{12,20},{16,8},{20,12},{24,0},{28,4},{1,25},{... | collective-permute-start | bytes 3145736 | tf_op jit(solution)/shard_map/ppermute | solution.py:197
  684.5 37.6 %collective-permute-start.21 = (bf16[128,2,1408]{2,0,1:T(8,128)(2,1)}, bf16[128,2,1408]{2,0,1:T(8,128)(2,1)}, u32[]{:S(2)}, u32[]{:S(2)}) collective-permute-start(bf16[128,2,1408]{2,0,1:T(8,128)(2,1)} %fusion.176), channel_id=1, source_target_pairs={{0,8},{4,12},{8,0},{12,4},{16,24},{20,28},{24,16},{28,20},{1,9},{5... | collective-permute-start | bytes 2162696 | tf_op jit(solution)/shard_map/ppermute | solution.py:197
  688.8 33.3 %collective-permute-start.23 = (bf16[128,2,1408]{2,0,1:T(8,128)(2,1)}, bf16[128,2,1408]{2,0,1:T(8,128)(2,1)}, u32[]{:S(2)}, u32[]{:S(2)}) collective-permute-start(bf16[128,2,1408]{2,0,1:T(8,128)(2,1)} %fusion.174), channel_id=1, source_target_pairs={{0,4},{4,0},{8,12},{12,8},{16,20},{20,16},{24,28},{28,24},{1,5},{5... | collective-permute-start | bytes 2162696 | tf_op jit(solution)/shard_map/ppermute | solution.py:197
  735.2 64.6 %collective-permute-start.5 = (bf16[256,4,512]{2,0,1:T(8,128)(2,1)}, bf16[256,4,512]{2,0,1:T(8,128)(2,1)}, u32[]{:S(2)}, u32[]{:S(2)}) collective-permute-start(bf16[256,4,512]{2,0,1:T(8,128)(2,1)} %pad_maximum_fusion.12), channel_id=1, source_target_pairs={{0,4},{4,0},{8,12},{12,8},{16,20},{20,16},{24,28},{28,24},{1,5},{5... | collective-permute-start | bytes 3145736 | tf_op jit(solution)/shard_map/ppermute | solution.py:197
  740.9 60.9 %collective-permute-start.7 = (bf16[256,4,512]{2,0,1:T(8,128)(2,1)}, bf16[256,4,512]{2,0,1:T(8,128)(2,1)}, u32[]{:S(2)}, u32[]{:S(2)}) collective-permute-start(bf16[256,4,512]{2,0,1:T(8,128)(2,1)} %pad_maximum_fusion.13), channel_id=1, source_target_pairs={{0,8},{4,12},{8,0},{12,4},{16,24},{20,28},{24,16},{28,20},{1,9},{5... | collective-permute-start | bytes 3145736 | tf_op jit(solution)/shard_map/ppermute | solution.py:197
  (178 other events, 1397.7 us)
Sparse Core Ops, SparseCore 0:
  159.4 39.8 all-gather.8
  201.5 38.8 all-gather.10
  290.2 49.0 all-reduce.28
  359.5 36.6 all-reduce.30
  398.1 46.8 all-gather.12
  473.6 43.5 all-gather.14
  695.5 51.0 all-reduce.32
